TPU v7x, 128 devices: a whole 4x4x4 slice. The times are simulated.
128 devices in a mesh: tok: 4 (over y), vocab: 32 (over x, z, core).
Axes of the slice: x: 4, y: 4, z: 4, core: 2. Of those that a mesh axis runs over, the one named last changes fastest.
Arguments:
- teacher_logits: bfloat16 [512, 131072], P('tok', 'vocab'), may hold values from -18 to 240
- hidden: bfloat16 [512, 4608], P('tok'), may hold values from -6 to 6
- new_head: bfloat16 [4608, 131072], P(None, ('tok', 'vocab')), may hold values from -0.26516504 to 0.26516504
- labels: int32 [512], replicated, may hold values from 0 to 131071
- map_target: int32 [1024, 4], P('vocab'), may hold values from 0 to 1023, as said below
- map_weight: bfloat16 [1024, 4, 128, 128], P('vocab'), may hold values from 0 to 0.017578125, as said below
Outputs:
- loss: float32 [512], P('tok')
- head_grad: bfloat16 [4608, 131072], P(None, ('tok', 'vocab'))
Inputs may be any that keep to these rules, and one draw needn't show every extreme that they name: `map_target`: values are ids of new blocks; new block b belongs to the device at index b // 8 of tok and vocab together, tok first. Of the 128 entries of one vocab index, at most 2 belong to one device, and some device gets exactly 2. `map_weight`: entries are non-negative.
All inputs are finite; a program needn't handle non-finite values.
Results may differ from a plain program's by a relative error of at most 0.001.
The roundings to bfloat16 on the way count: a program that leaves them out, or rounds other values in their place, can miss the bound.
Values may be sent and summed in bfloat16 or wider, within the bound.
A program may use at most 128 MiB of HBM per device.

v0:
```python
import jax
import jax.numpy as jnp
from jax import lax
from jax.sharding import PartitionSpec as P


def local(teacher_logits, hidden, new_head, labels, map_target, map_weight):
    tok_rows = teacher_logits.shape[0]
    block = map_weight.shape[2]
    fanout = map_weight.shape[1]
    old_blocks = map_target.shape[0]
    entries = old_blocks * fanout
    n_tok = lax.axis_size("tok")
    n_vocab = lax.axis_size("vocab")
    nodes = n_tok * n_vocab
    capacity = max(2, 2 * entries // nodes)
    new_cols = new_head.shape[1]
    per_node = new_cols // block
    own_index = lax.axis_index(("tok", "vocab"))
    scores = teacher_logits.astype(jnp.float32)
    local_top = jnp.max(scores, axis=1)
    highest = lax.pmax(local_top, "vocab")
    total = lax.psum(jnp.sum(jnp.exp(scores - highest[:, None]), axis=1), "vocab")
    teacher_prob = (jnp.exp(scores - highest[:, None]) / total[:, None]).astype(jnp.bfloat16)
    pieces = teacher_prob.reshape(tok_rows, old_blocks, block)
    contrib = jnp.einsum("tjb,jkbc->jktc", pieces, map_weight, preferred_element_type=jnp.float32)
    contrib = contrib.astype(jnp.bfloat16).reshape(entries, tok_rows, block)
    owners = (map_target // per_node).reshape(entries)
    earlier = jnp.arange(entries)[None, :] < jnp.arange(entries)[:, None]
    slots = jnp.sum((owners[:, None] == owners[None, :]) & earlier, axis=1)
    outbox = (
        jnp.zeros((nodes, capacity, tok_rows, block), jnp.bfloat16).at[owners, slots].set(contrib)
    )
    inbox = lax.all_to_all(outbox, ("tok", "vocab"), split_axis=0, concat_axis=0, tiled=True)
    inbox = inbox.reshape(n_tok, n_vocab, capacity, tok_rows, block)
    targets_all = lax.all_gather(map_target, "vocab", axis=0, tiled=True).reshape(n_vocab, entries)
    owners_all = targets_all // per_node
    local_block = targets_all % per_node
    slots_all = jnp.sum((owners_all[:, :, None] == owners_all[:, None, :]) & earlier[None], axis=2)
    picked = (owners_all == own_index)[:, :, None] & (
        slots_all[:, :, None] == jnp.arange(capacity)[None, None, :]
    )
    block_hit = local_block[:, :, None] == jnp.arange(per_node)[None, None, :]
    landing = jnp.einsum(
        "vec,veb->vcb", picked.astype(jnp.float32), block_hit.astype(jnp.float32)
    ).astype(jnp.bfloat16)
    target = jnp.einsum("vcb,svctk->stbk", landing, inbox, preferred_element_type=jnp.float32)
    target = target.reshape(n_tok * tok_rows, new_cols)
    everyone = lax.all_gather(hidden, "tok", axis=0, tiled=True)
    logits = jnp.dot(everyone, new_head, preferred_element_type=jnp.float32)
    columns = own_index * new_cols + jnp.arange(new_cols, dtype=jnp.int32)
    label_hit = labels[:, None] == columns[None, :]
    label_part = jnp.sum(jnp.where(label_hit, logits, 0.0), axis=1)
    mass_part = jnp.sum(target, axis=1)
    inner_part = jnp.sum(target * logits, axis=1)
    row_top = jnp.max(logits, axis=1)
    top_all = lax.pmax(row_top, ("tok", "vocab"))
    exp_part = jnp.sum(jnp.exp(logits - top_all[:, None]), axis=1)
    total_all, target_mass, inner, label_logit = lax.psum(
        (exp_part, mass_part, inner_part, label_part), ("tok", "vocab")
    )
    log_total = top_all + jnp.log(total_all)
    loss_all = target_mass * log_total - inner + log_total - label_logit
    loss = lax.dynamic_slice_in_dim(loss_all, lax.axis_index("tok") * tok_rows, tok_rows)
    probs = jnp.exp(logits - log_total[:, None])
    grad_logits = (
        (target_mass + 1.0)[:, None] * probs - target - label_hit.astype(jnp.float32)
    ).astype(jnp.bfloat16)
    head_grad = lax.dot_general(
        everyone, grad_logits, (((0,), (0,)), ((), ())), preferred_element_type=jnp.float32
    )
    return (loss, head_grad.astype(jnp.bfloat16))


def solution(mesh):
    return jax.shard_map(
        local,
        mesh=mesh,
        in_specs=(
            P("tok", "vocab"),
            P("tok", None),
            P(None, ("tok", "vocab")),
            P(),
            P("vocab", None),
            P("vocab", None, None, None),
        ),
        out_specs=(P("tok"), P(None, ("tok", "vocab"))),
        check_vma=False,
    )
```

profile of v0, /device:TPU:1, one launch (start us, length us, event | category | flops | bytes accessed | tf_op | source)
XLA Modules:
  0.0 477.8 jit_solution(10782458382185194525)
XLA Ops:
  7.2 0.0 copy-start
  7.2 0.0 all-gather.3.cloned.1.call-start
  7.2 0.7 all-gather.3.cloned.1.call-update
  7.9 0.7 add_select_fusion.2
  8.6 0.1 copy.44
  8.7 0.1 eq.79
  8.8 0.1 reshape.176
  8.9 1.5 reduce_max.23
  10.4 64.8 %pmax.14 = f32[128]{0:T(128)S(1)} all-reduce(bf16[128]{0:T(256)(128)(2,1)S(1)} %reduce_max.23), channel_id=1, replica_groups=mesh['tok'=4,'vocab'=32] {'vocab'}, use_global_device_ids=true, to_apply=%region_2.0 | all-reduce | flops 128 | bytes 768 | tf_op jit(solution)/shard_map/pmax | solution.py:22
  75.2 0.0 copy-done
  75.2 0.5 fusion.7
  75.7 67.0 %psum.35 = f32[128]{0:T(128)S(1)} all-reduce(f32[128]{0:T(128)S(1)} %fusion.7), channel_id=1, replica_groups=mesh['tok'=4,'vocab'=32] {'vocab'}, use_global_device_ids=true, to_apply=%region_4.5 | all-reduce | flops 128 | bytes 1024 | tf_op jit(solution)/shard_map/psum | solution.py:23
  142.7 0.0 copy-start.2
  142.7 0.5 fusion.9
  143.2 0.2 copy.62
  143.5 0.2 convert_reduce_fusion.1
  143.6 1.3 copy-done.2
  144.9 3.2 convolution_convert_fusion.1
  148.1 5.5 %broadcast_in_dim.5 = bf16[128,2,128,128]{3,2,1,0:T(8,128)(2,1)} broadcast(bf16[]{:T(256)} %constant.50.clone.1), dimensions={} | broadcast | bytes 8388610 | tf_op jit(solution)/shard_map/broadcast_in_dim | solution.py:32
  153.6 20.7 %scatter_fusion = bf16[128,2,128,128]{3,2,1,0:T(8,128)(2,1)} fusion(bf16[128,2,128,128]{3,2,1,0:T(8,128)(2,1)} %broadcast_in_dim.5, s32[128]{0:T(128)S(1)} %fusion.26, bf16[128,128,128]{2,1,0:T(8,128)(2,1)} %bitcast.43), kind=kCustom, calls=%fused_computation | custom fusion | bytes 12583936 | tf_op jit(solution)/shard_map/scatter | solution.py:32
  174.4 0.0 copy-start.4
  174.4 5.4 %all-to-all-start = ((bf16[128,2,128,128]{3,2,1,0:T(8,128)(2,1)}), bf16[128,2,128,128]{3,2,1,0:T(8,128)(2,1)}, u32[]{:S(2)}, u32[]{:S(2)}) async-start(bf16[128,2,128,128]{3,2,1,0:T(8,128)(2,1)} %scatter_fusion), calls=%async_computation | async-start | bytes 16777216 | tf_op jit(solution)/shard_map/all_to_all | solution.py:34
  179.8 0.0 copy-done.4
  179.8 117.2 %all-gather = s32[32,32,4]{1,2,0:T(4,128)S(1)} all-gather(s32[1,32,4]{1,2,0:T(4,128)S(1)} %bitcast.47), channel_id=1, replica_groups=mesh['tok'=4,'vocab'=32] {'vocab'}, dimensions={0}, use_global_device_ids=true | all-gather | bytes 16896 | tf_op jit(solution)/shard_map/all_gather | solution.py:36
  297.0 0.1 copy.47
  297.1 0.1 copy.48
  297.2 1.3 convert_reduce_fusion
  298.5 0.2 fusion.8
  298.7 0.0 all-gather.3.cloned.1.call-done
  298.7 10.1 %fusion.27 = (f32[512]{0:T(512)S(1)}, f32[512,1024]{1,0:T(8,128)}) fusion(bf16[512,4608]{1,0:T(8,128)(2,1)} %all-gather.3.cloned.1.call-done, bf16[4608,1024]{1,0:T(8,128)(2,1)} %param.8), kind=kOutput, calls=%fused_computation.64 | convolution fusion | flops 4832361984 | bytes 16254976 | tf_op jit(solution)/shard_map/dot_general | solution.py:50
  308.8 65.0 %pmax.15 = f32[512]{0:T(512)S(1)} all-reduce(f32[512]{0:T(512)S(1)} %get-tuple-element.24), channel_id=1, replica_groups=mesh['tok'=4,'vocab'=32] {'tok','vocab'}, use_global_device_ids=true, to_apply=%region_10.11 | all-reduce | flops 512 | bytes 4096 | tf_op jit(solution)/shard_map/pmax | solution.py:57
  373.8 0.0 all-to-all-done
  373.8 0.0 copy-start.1
  373.9 0.0 copy-start.3
  373.9 8.9 %bitcast_reduce_fusion = (f32[4,128]{1,0:T(4,128)S(1)}, f32[4,128,128,8,1]{2,3,4,1,0:T(8,128)S(1)}) fusion(bf16[32,2,8,1,1]{2,1,0,4,3:T(2,128)(2,1)S(1)} %fusion.8, bf16[4,32,2,128,128]{4,3,2,1,0:T(8,128)(2,1)} %bitcast.5), kind=kOutput, calls=%fused_computation.14 | convolution fusion | flops 67632640 | bytes 10488832 | tf_op jit(solution)/shard_map/vcb,svctk->stbk/dot_general | solution.py:47
  382.8 0.0 copy-done.1
  382.8 0.0 copy-done.3
  382.8 1.2 fusion.6
  384.0 62.9 %all-reduce = (f32[512]{0:T(512)S(1)}, f32[512]{0:T(512)S(1)}, f32[512]{0:T(512)S(1)}, f32[512]{0:T(512)S(1)}) all-reduce(f32[512]{0:T(512)S(1)} %get-tuple-element.13, f32[512]{0:T(512)S(1)} %get-tuple-element.14, f32[512]{0:T(512)S(1)} %get-tuple-element.12, f32[512]{0:T(512)S(1)} %bitcast.46), channel_id=1, replica_groups=mesh['tok'=4,'vocab'=32] {'tok','vocab'}, use_global_device_ids=true, to_apply=%region_16.17 | all-reduce | flops 2048 | bytes 16384 | tf_op jit(solution)/shard_map/psum | solution.py:59
  446.8 10.9 %fusion.2 = bf16[4608,1024]{0,1:T(8,128)(2,1)} fusion(bf16[512,4608]{1,0:T(8,128)(2,1)} %all-gather.3.cloned.1.call-done, f32[512,1024]{1,0:T(8,128)} %get-tuple-element.25, f32[64,8,8,128]{3,2,1,0:T(8,128)S(1)} %bitcast.42, f32[512]{0:T(512)S(1)} %get-tuple-element.20, f32[512]{0:T(512)S(1)} %get-tuple-element.23, s32[1024]{0:T(1024)S(1)} %iota_add_fusion, ...), kind=kOutput, calls=%fused_computation.4 | convolution fusion | flops 4840226816 | bytes 18360320 | tf_op jit(solution)/shard_map/dot_general | solution.py:69
  457.8 12.6 %copy.54 = bf16[4608,1024]{1,0:T(8,128)(2,1)} copy(bf16[4608,1024]{0,1:T(8,128)(2,1)} %fusion.2) | data formatting | bytes 18874368
  470.4 0.6 dynamic_slice.3
  (6 shorter events, 0.1 us)
Async XLA Ops:
  7.2 68.0 %copy-start = (bf16[128,4096]{1,0:T(8,128)(2,1)S(1)}, bf16[128,4096]{1,0:T(8,128)(2,1)}, u32[]{:S(2)}) copy-start(bf16[128,4096]{1,0:T(8,128)(2,1)} %param.6) | copy-start | bytes 3145732
  7.2 291.5 %all-gather.3.cloned.1.call-start = ((), (), s32[]{:S(2)}) async-start(), calls=%async_computation.1 | async-start | bytes 5898240 | tf_op jit(solution)/shard_map/all_gather | solution.py:49
  142.7 2.2 copy-start.2
  174.4 5.4 %copy-start.4 = (s32[32,4]{0,1:T(4,128)S(1)}, s32[32,4]{0,1:T(4,128)}, u32[]{:S(2)}) copy-start(s32[32,4]{0,1:T(4,128)} %param.10) | copy-start | bytes 1540
  174.4 199.5 %all-to-all-start = ((bf16[128,2,128,128]{3,2,1,0:T(8,128)(2,1)}), bf16[128,2,128,128]{3,2,1,0:T(8,128)(2,1)}, u32[]{:S(2)}, u32[]{:S(2)}) async-start(bf16[128,2,128,128]{3,2,1,0:T(8,128)(2,1)} %scatter_fusion), calls=%async_computation | async-start | bytes 16777216 | tf_op jit(solution)/shard_map/all_to_all | solution.py:34
  373.8 8.9 %copy-start.1 = (f32[512,1024]{1,0:T(8,128)S(1)}, f32[512,1024]{1,0:T(8,128)}, u32[]{:S(2)}) copy-start(f32[512,1024]{1,0:T(8,128)} %get-tuple-element.25) | copy-start | bytes 6291460
  373.9 8.9 %copy-start.3 = (s32[512]{0:T(512)S(1)}, s32[512]{0:T(512)}, u32[]{:S(2)}) copy-start(s32[512]{0:T(512)} %param.9) | copy-start | bytes 6148
Sparse Core Ops, SparseCore 0:
  9.7 55.8 all-gather.2
where the time goes:
time: 479 us; the launch traced here: 478 us
  blocking collectives  377 us (79%)
  local copies, waits for them, and re-layouts  41.4 us (9%)
  matrix products  33.3 us (7%)
  between operations  14.2 us (3%)
  other arithmetic  5.87 us (1%)
  starting transfers between devices  5.46 us (1%)
    all_gather x1, blocking collectives, local(): lax.all_gather(map_target, 'vocab', axis=0, tiled=True)  117 us
    psum x1, blocking collectives, local(): lax.psum(jnp.sum(jnp.exp(scores - highest[:, None]), axis=1), 'vocab')  67 us
    pmax x1, blocking collectives, local(): top_all = lax.pmax(row_top, ('tok', 'vocab'))  65 us
    pmax x1, blocking collectives, local(): highest = lax.pmax(local_top, 'vocab')  64.8 us
    psum x1, blocking collectives, local(): lax.psum((exp_part, mass_part, inner_part, label_part), ('tok', 'vocab'))  62.9 us
    scatter x1, local copies, waits for them, and re-layouts, local(): jnp.zeros((nodes, capacity, tok_rows, block), jnp.bfloat16)  20.7 us
    unnamed x12, local copies, waits for them, and re-layouts  14.1 us
    dot_general x1, matrix products, local(): lax.dot_general(everyone, grad_logits, (((0,), (0,)), ((), ())), preferre...  10.9 us
  transfers between devices with their start and end apart: 2, of which 0 were waited for; matrix products, arithmetic and copies ran while one was open for 9% of the time, Pallas kernels for 0%

commit v1 on v0

--- a/solution.py
+++ b/solution.py
@@ -1,7 +1,19 @@
+import functools
 import jax
 import jax.numpy as jnp
 from jax import lax
 from jax.sharding import PartitionSpec as P
+
+
+def tasks_draw(xs, lane_axis):
+    before = lax.axis_size(lane_axis)
+    local_part = jnp.stack(before * [xs], 0)
+    finding = lax.all_to_all(local_part, lane_axis, concat_axis=0, split_axis=0)
+    arr_out = jnp.concatenate(finding, 0)
+    return arr_out
+
+
+perform_the_joints = functools.partial(tasks_draw, lane_axis="vocab")
 
 
 def local(teacher_logits, hidden, new_head, labels, map_target, map_weight):
@@ -33,7 +45,7 @@
     )
     inbox = lax.all_to_all(outbox, ("tok", "vocab"), split_axis=0, concat_axis=0, tiled=True)
     inbox = inbox.reshape(n_tok, n_vocab, capacity, tok_rows, block)
-    targets_all = lax.all_gather(map_target, "vocab", axis=0, tiled=True).reshape(n_vocab, entries)
+    targets_all = perform_the_joints(map_target).reshape(n_vocab, entries)
     owners_all = targets_all // per_node
     local_block = targets_all % per_node
     slots_all = jnp.sum((owners_all[:, :, None] == owners_all[:, None, :]) & earlier[None], axis=2)

time: 479 us -> 452 us (0.944)
  blocking collectives: 377 us -> 339 us
  starting transfers between devices: 5.46 us -> 14.8 us
    all_gather x1 -> x0, blocking collectives: 117 us -> none  [local(): lax.all_gather(map_target, 'vocab', axis=0, tiled=True)]
    pmax x1, blocking collectives: 65 us -> 144 us  [local(): top_all = lax.pmax(row_top, ('tok', 'vocab'))]
    all_to_all x0 -> x1, starting transfers between devices: none -> 9.43 us  [tasks_draw(): finding = lax.all_to_all(local_part, lane_axis, concat_axis=0, split_axis=0)]
    unnamed x12 -> x13, local copies, waits for them, and re-layouts: 14.1 us -> 15.7 us
  transfers between devices with their start and end apart: 2 -> 3, of which waited for: 0 -> 0; matrix products, arithmetic and copies ran while one was open for 9% -> 10% of each run, Pallas kernels for 0% -> 0%
where the time goes in v1:
time: 452 us; the launch traced here: 451 us
  blocking collectives  339 us (75%)
  local copies, waits for them, and re-layouts  43.5 us (10%)
  matrix products  33.3 us (7%)
  starting transfers between devices  14.8 us (3%)
  between operations  14.2 us (3%)
  other arithmetic  5.33 us (1%)
    pmax x1, blocking collectives, local(): top_all = lax.pmax(row_top, ('tok', 'vocab'))  144 us
    psum x1, blocking collectives, local(): lax.psum(jnp.sum(jnp.exp(scores - highest[:, None]), axis=1), 'vocab')  67.4 us
    psum x1, blocking collectives, local(): lax.psum((exp_part, mass_part, inner_part, label_part), ('tok', 'vocab'))  64.8 us
    pmax x1, blocking collectives, local(): highest = lax.pmax(local_top, 'vocab')  62.5 us
    scatter x1, local copies, waits for them, and re-layouts, local(): jnp.zeros((nodes, capacity, tok_rows, block), jnp.bfloat16)  20.7 us
    unnamed x13, local copies, waits for them, and re-layouts  15.7 us
    dot_general x1, matrix products, local(): lax.dot_general(everyone, grad_logits, (((0,), (0,)), ((), ())), preferre...  11 us
    dot_general x1, matrix products, local(): logits = jnp.dot(everyone, new_head, preferred_element_type=jnp.float32)  10.1 us
  transfers between devices with their start and end apart: 3, of which 0 were waited for; matrix products, arithmetic and copies ran while one was open for 10% of the time, Pallas kernels for 0%

profile of v1, /device:TPU:1, one launch (start us, length us, event | category | flops | bytes accessed | tf_op | source)
XLA Modules:
  0.0 450.8 jit_solution(8474738600645579342)
XLA Ops:
  7.2 0.0 copy-start
  7.2 0.8 broadcast_bitcast_fusion
  8.0 0.7 reshape.189
  8.7 9.4 %all-to-all-start.1 = ((s32[32,1,128]{2,1,0:T(1,128)}), s32[32,1,128]{2,1,0:T(1,128)S(1)}, u32[]{:S(2)}, u32[]{:S(2)}) async-start(s32[32,1,128]{2,1,0:T(1,128)} %reshape.189), calls=%async_computation.1 | async-start | bytes 32768 | tf_op jit(solution)/shard_map/all_to_all | solution.py:11
  18.1 0.0 all-gather.2.cloned.1.call-start
  18.1 0.7 all-gather.2.cloned.1.call-update
  18.8 0.7 add_select_fusion.2
  19.5 0.1 copy.57
  19.6 0.1 eq.79
  19.7 0.1 reshape.175
  19.8 0.0 copy-done
  19.8 0.2 reduce_max.23
  20.1 62.5 %pmax.14 = f32[128]{0:T(128)S(1)} all-reduce(bf16[128]{0:T(256)(128)(2,1)S(1)} %reduce_max.23), channel_id=1, replica_groups=mesh['tok'=4,'vocab'=32] {'vocab'}, use_global_device_ids=true, to_apply=%region_2.0 | all-reduce | flops 128 | bytes 768 | tf_op jit(solution)/shard_map/pmax | solution.py:34
  82.6 0.5 fusion.7
  83.1 67.4 %psum.35 = f32[128]{0:T(128)S(1)} all-reduce(f32[128]{0:T(128)S(1)} %fusion.7), channel_id=1, replica_groups=mesh['tok'=4,'vocab'=32] {'vocab'}, use_global_device_ids=true, to_apply=%region_4.5 | all-reduce | flops 128 | bytes 1024 | tf_op jit(solution)/shard_map/psum | solution.py:35
  150.4 0.0 copy-start.2
  150.4 0.5 fusion.9
  150.9 0.2 copy.75
  151.2 0.2 convert_reduce_fusion.1
  151.4 1.3 copy-done.2
  152.6 3.2 convolution_convert_fusion.1
  155.8 5.5 %broadcast_in_dim.5 = bf16[128,2,128,128]{3,2,1,0:T(8,128)(2,1)} broadcast(bf16[]{:T(256)} %constant.50.clone.1), dimensions={} | broadcast | bytes 8388610 | tf_op jit(solution)/shard_map/broadcast_in_dim | solution.py:44
  161.4 20.7 %scatter_fusion = bf16[128,2,128,128]{3,2,1,0:T(8,128)(2,1)} fusion(bf16[128,2,128,128]{3,2,1,0:T(8,128)(2,1)} %broadcast_in_dim.5, s32[128]{0:T(128)S(1)} %fusion.26, bf16[128,128,128]{2,1,0:T(8,128)(2,1)} %bitcast.45), kind=kCustom, calls=%fused_computation | custom fusion | bytes 12583936 | tf_op jit(solution)/shard_map/scatter | solution.py:44
  182.1 0.0 all-to-all-done.1
  182.1 5.3 %all-to-all-start = ((bf16[128,2,128,128]{3,2,1,0:T(8,128)(2,1)}), bf16[128,2,128,128]{3,2,1,0:T(8,128)(2,1)}, u32[]{:S(2)}, u32[]{:S(2)}) async-start(bf16[128,2,128,128]{3,2,1,0:T(8,128)(2,1)} %scatter_fusion), calls=%async_computation | async-start | bytes 16777216 | tf_op jit(solution)/shard_map/all_to_all | solution.py:46
  187.4 0.5 broadcast.187
  187.9 0.7 reduce.2
  188.6 0.1 reshape.190
  188.7 0.1 copy.60
  188.8 0.1 copy.61
  188.9 1.3 convert_reduce_fusion
  190.3 0.2 fusion.8
  190.4 0.0 all-gather.2.cloned.1.call-done
  190.5 10.1 %fusion.27 = (f32[512]{0:T(512)S(1)}, f32[512,1024]{1,0:T(8,128)}) fusion(bf16[512,4608]{1,0:T(8,128)(2,1)} %all-gather.2.cloned.1.call-done, bf16[4608,1024]{1,0:T(8,128)(2,1)} %param.8), kind=kOutput, calls=%fused_computation.64 | convolution fusion | flops 4832361984 | bytes 16254976 | tf_op jit(solution)/shard_map/dot_general | solution.py:62
  200.5 144.3 %pmax.15 = f32[512]{0:T(512)S(1)} all-reduce(f32[512]{0:T(512)S(1)} %get-tuple-element.26), channel_id=1, replica_groups=mesh['tok'=4,'vocab'=32] {'tok','vocab'}, use_global_device_ids=true, to_apply=%region_10.11 | all-reduce | flops 512 | bytes 4096 | tf_op jit(solution)/shard_map/pmax | solution.py:69
  344.9 0.0 all-to-all-done
  344.9 0.0 copy-start.1
  344.9 0.0 copy-start.3
  344.9 8.9 %bitcast_reduce_fusion = (f32[4,128]{1,0:T(4,128)S(1)}, f32[4,128,128,8,1]{2,3,4,1,0:T(8,128)S(1)}) fusion(bf16[32,2,8,1,1]{2,1,0,4,3:T(2,128)(2,1)S(1)} %fusion.8, bf16[4,32,2,128,128]{4,3,2,1,0:T(8,128)(2,1)} %bitcast.5), kind=kOutput, calls=%fused_computation.14 | convolution fusion | flops 67632640 | bytes 10488832 | tf_op jit(solution)/shard_map/vcb,svctk->stbk/dot_general | solution.py:59
  353.8 0.0 copy-done.1
  353.8 0.0 copy-done.3
  353.8 1.2 fusion.6
  355.0 64.8 %all-reduce = (f32[512]{0:T(512)S(1)}, f32[512]{0:T(512)S(1)}, f32[512]{0:T(512)S(1)}, f32[512]{0:T(512)S(1)}) all-reduce(f32[512]{0:T(512)S(1)} %get-tuple-element.15, f32[512]{0:T(512)S(1)} %get-tuple-element.16, f32[512]{0:T(512)S(1)} %get-tuple-element.14, f32[512]{0:T(512)S(1)} %bitcast.49), channel_id=1, replica_groups=mesh['tok'=4,'vocab'=32] {'tok','vocab'}, use_global_device_ids=true, to_apply=%region_16.17 | all-reduce | flops 2048 | bytes 16384 | tf_op jit(solution)/shard_map/psum | solution.py:71
  419.8 11.0 %fusion.2 = bf16[4608,1024]{0,1:T(8,128)(2,1)} fusion(bf16[512,4608]{1,0:T(8,128)(2,1)} %all-gather.2.cloned.1.call-done, f32[512,1024]{1,0:T(8,128)} %get-tuple-element.27, f32[64,8,8,128]{3,2,1,0:T(8,128)S(1)} %bitcast.44, f32[512]{0:T(512)S(1)} %get-tuple-element.22, f32[512]{0:T(512)S(1)} %get-tuple-element.25, s32[1024]{0:T(1024)S(1)} %iota_add_fusion, ...), kind=kOutput, calls=%fused_computation.4 | convolution fusion | flops 4840226816 | bytes 18360320 | tf_op jit(solution)/shard_map/dot_general | solution.py:81
  430.8 12.6 %copy.67 = bf16[4608,1024]{1,0:T(8,128)(2,1)} copy(bf16[4608,1024]{0,1:T(8,128)(2,1)} %fusion.2) | data formatting | bytes 18874368
  443.4 0.6 dynamic_slice.3
  (6 shorter events, 0.1 us)
Async XLA Ops:
  7.2 12.7 %copy-start = (bf16[128,4096]{1,0:T(8,128)(2,1)S(1)}, bf16[128,4096]{1,0:T(8,128)(2,1)}, u32[]{:S(2)}) copy-start(bf16[128,4096]{1,0:T(8,128)(2,1)} %param.6) | copy-start | bytes 3145732
  8.7 173.4 %all-to-all-start.1 = ((s32[32,1,128]{2,1,0:T(1,128)}), s32[32,1,128]{2,1,0:T(1,128)S(1)}, u32[]{:S(2)}, u32[]{:S(2)}) async-start(s32[32,1,128]{2,1,0:T(1,128)} %reshape.189), calls=%async_computation.1 | async-start | bytes 32768 | tf_op jit(solution)/shard_map/all_to_all | solution.py:11
  18.1 172.3 %all-gather.2.cloned.1.call-start = ((), (), s32[]{:S(2)}) async-start(), calls=%async_computation.2 | async-start | bytes 5898240 | tf_op jit(solution)/shard_map/all_gather | solution.py:61
  150.4 2.2 copy-start.2
  182.1 162.8 %all-to-all-start = ((bf16[128,2,128,128]{3,2,1,0:T(8,128)(2,1)}), bf16[128,2,128,128]{3,2,1,0:T(8,128)(2,1)}, u32[]{:S(2)}, u32[]{:S(2)}) async-start(bf16[128,2,128,128]{3,2,1,0:T(8,128)(2,1)} %scatter_fusion), calls=%async_computation | async-start | bytes 16777216 | tf_op jit(solution)/shard_map/all_to_all | solution.py:46
  344.9 8.9 %copy-start.1 = (f32[512,1024]{1,0:T(8,128)S(1)}, f32[512,1024]{1,0:T(8,128)}, u32[]{:S(2)}) copy-start(f32[512,1024]{1,0:T(8,128)} %get-tuple-element.27) | copy-start | bytes 6291460
  344.9 8.9 %copy-start.3 = (s32[512]{0:T(512)S(1)}, s32[512]{0:T(512)}, u32[]{:S(2)}) copy-start(s32[512]{0:T(512)} %param.9) | copy-start | bytes 6148
Sparse Core Ops, SparseCore 0:
  20.6 53.7 all-gather.1
